TPU v7x, 256 devices: a whole 4x4x8 slice. The times are simulated.
256 devices in a mesh: row: 8 (over y, core), col: 32 (over z, x).
Axes of the slice: x: 4, y: 4, z: 8, core: 2. Of those that a mesh axis runs over, the one named last changes fastest.
Arguments:
- probes: bfloat16 [32, 8, 128, 4096], P(None, None, 'row', 'col'), may hold values from -8 to 8
- spread: float32 [8, 128, 4096], P(None, 'row', 'col'), may hold values from 0.05 to 6.5, as said below
- adv_x: float32 [8, 128, 4096], P(None, 'row', 'col'), may hold values from -0.6 to 0.6
- adv_y: float32 [8, 128, 4096], P(None, 'row', 'col'), may hold values from -0.6 to 0.6
- diffusivity: float32 [8, 128, 4096], P(None, 'row', 'col'), may hold values from 0.02 to 0.2
Outputs:
- basis: float32 [32, 8, 128, 4096], P(None, None, 'row', 'col')
- core_factor: float32 [32, 32], replicated
Inputs may be any that keep to these rules, and one draw needn't show every extreme that they name: `spread`: positive everywhere; a rough factor times a scale that varies over the grid.
All inputs are finite; a program needn't handle non-finite values.
Results may differ from a plain program's by a relative error of at most 0.0003.
Values sent between devices are 32-bit elements; how exact they have to be, the bound alone decides.
A program may use at most 128 MiB of HBM per device.

v0:
```python
import jax
import jax.numpy as jnp
from jax import lax
from jax.sharding import PartitionSpec as P


def padded_2(block, sides, width):
    for axis, dim in sides:
        count = lax.axis_size(axis)
        forward = [(i, i + 1) for i in range(count - 1)]
        backward = [(target, source) for source, target in forward]
        low = lax.ppermute(
            lax.slice_in_dim(block, block.shape[dim] - width, None, axis=dim), axis, forward
        )
        high = lax.ppermute(lax.slice_in_dim(block, 0, width, axis=dim), axis, backward)
        block = jnp.concatenate([low, block, high], axis=dim)
    return block


def shifted(padded, dx, dy):
    nx = padded.shape[-2] - 4
    ny = padded.shape[-1] - 4
    return padded[..., 2 + dx : 2 + dx + nx, 2 + dy : 2 + dy + ny]


def first_diff(padded, axis_id):
    if axis_id == 0:
        return (
            -shifted(padded, 2, 0)
            + 8.0 * shifted(padded, 1, 0)
            - 8.0 * shifted(padded, -1, 0)
            + shifted(padded, -2, 0)
        ) / 12.0
    return (
        -shifted(padded, 0, 2)
        + 8.0 * shifted(padded, 0, 1)
        - 8.0 * shifted(padded, 0, -1)
        + shifted(padded, 0, -2)
    ) / 12.0


def laplace(padded):
    return (
        shifted(padded, 1, 0)
        + shifted(padded, -1, 0)
        + shifted(padded, 0, 1)
        + shifted(padded, 0, -1)
        - 4.0 * shifted(padded, 0, 0)
    )


def vertical(center):
    upper = jnp.concatenate([center[:, 1:], center[:, -1:]], axis=1)
    lower = jnp.concatenate([center[:, :1], center[:, :-1]], axis=1)
    return upper + lower - 2.0 * center


def tangent(padded, coef_x, coef_y, coef_d):
    center = shifted(padded, 0, 0)
    return (
        center
        + coef_x * first_diff(padded, 0)
        + coef_y * first_diff(padded, 1)
        + coef_d * laplace(padded)
        + 0.2 * vertical(center)
    )


def adjoint(padded, pad_x, pad_y, pad_d):
    center = shifted(padded, 0, 0)
    return (
        center
        - first_diff(pad_x * padded, 0)
        - first_diff(pad_y * padded, 1)
        + laplace(pad_d * padded)
        + 0.2 * vertical(center)
    )


def lower_chol(matrix):
    order = matrix.shape[0]
    lower = jnp.zeros_like(matrix)
    for col_id in range(order):
        resid = matrix[:, col_id] - jnp.dot(
            lower, lower[col_id, :], precision=lax.Precision.HIGHEST
        )
        pivot = jnp.sqrt(resid[col_id])
        below = jnp.arange(order) > col_id
        column = jnp.where(below, resid / pivot, jnp.float32(0.0))
        column = column.at[col_id].set(pivot)
        lower = lower.at[:, col_id].set(column)
    return lower


def lower_inverse(lower):
    order = lower.shape[0]
    eye = jnp.eye(order, dtype=jnp.float32)
    result = jnp.zeros_like(lower)
    for row_id in range(order):
        line = (
            eye[row_id] - jnp.dot(lower[row_id], result, precision=lax.Precision.HIGHEST)
        ) / lower[row_id, row_id]
        result = result.at[row_id].set(line)
    return result


def factors(gram, core):
    gram = 0.5 * (gram + gram.T)
    core = 0.5 * (core + core.T)
    low_gram = lower_chol(gram)
    upper = low_gram.T
    inv_upper = lower_inverse(low_gram).T
    low_core = lower_chol(core)
    inv_low = lower_inverse(low_core)
    factor = jnp.dot(upper, inv_low.T, precision=lax.Precision.HIGHEST)
    return (inv_upper, factor)


def shards(probes, spread, adv_x, adv_y, diffusivity):
    nprobe, nlev, rows_here, cols_here = probes.shape
    stacked = jnp.stack([adv_x, adv_y, diffusivity])
    coef_pad = padded_2(stacked, (("row", 2), ("col", 3)), 2)
    pad_x = coef_pad[0]
    pad_y = coef_pad[1]
    pad_d = coef_pad[2]
    omega = probes.astype(jnp.float32)
    scaled = spread * omega
    scaled_pad = padded_2(scaled, (("row", 2), ("col", 3)), 2)
    tang = tangent(scaled_pad, adv_x, adv_y, diffusivity)
    tang_pad = padded_2(tang, (("row", 2), ("col", 3)), 2)
    back = adjoint(tang_pad, pad_x, pad_y, pad_d)
    sketch = omega + spread * back
    flat = sketch.reshape(nprobe, -1)
    omega_flat = omega.reshape(nprobe, -1)
    gram_part = jnp.dot(flat, flat.T, precision=lax.Precision.HIGHEST)
    core_part = jnp.dot(omega_flat, flat.T, precision=lax.Precision.HIGHEST)
    gram, core = lax.psum((gram_part, core_part), ("row", "col"))
    inv_upper, factor = factors(gram, core)
    count = float(nlev * rows_here * cols_here * lax.axis_size("row") * lax.axis_size("col"))
    basis = jnp.dot(inv_upper.T, flat, precision=lax.Precision.HIGHEST) * jnp.sqrt(
        jnp.float32(count)
    )
    return (basis.reshape(nprobe, nlev, rows_here, cols_here), factor)


def solution(mesh):
    return jax.shard_map(
        shards,
        mesh=mesh,
        in_specs=(
            P(None, None, "row", "col"),
            P(None, "row", "col"),
            P(None, "row", "col"),
            P(None, "row", "col"),
            P(None, "row", "col"),
        ),
        out_specs=(P(None, None, "row", "col"), P()),
        check_vma=False,
    )
```

profile of v0, /device:TPU:1, one launch (start us, length us, event | category | flops | bytes accessed | tf_op | source)
XLA Modules:
  0.0 503.2 jit_solution(10391546378540599181)
XLA Ops:
  1.5 1.6 convert_multiply_fusion
  3.2 5.1 %collective-permute-start = (f32[32,8,2,128]{3,1,2,0:T(8,128)S(1)}, f32[32,8,2,128]{3,1,2,0:T(8,128)S(1)}, u32[]{:S(2)}, u32[]{:S(2)}) collective-permute-start(f32[32,8,2,128]{3,1,2,0:T(8,128)S(1)} %get-tuple-element.2454), channel_id=1, source_target_pairs={{32,0},{64,32},{96,64},{128,96},{160,128},{192,160},{224,192},{33,... | collective-permute-start | bytes 786440 | tf_op jit(solution)/shard_map/ppermute | solution.py:15
  8.4 1.9 collective-permute-start.1
  10.3 1.9 collective-permute-start.4
  12.3 2.4 collective-permute-start.5
  14.7 2.5 fusion.515
  18.5 2.6 collective-permute-start.6
  46.9 2.5 fusion.510
  49.4 3.6 copy.44
  54.3 2.0 copy.46
  56.3 4.9 collective-permute-start.3
  64.5 4.4 copy.45
  69.0 3.5 copy.47
  72.5 13.8 %fusion.10 = f32[32,8,16,128]{3,1,2,0:T(8,128)S(1)} fusion(f32[32,8,16,128]{3,1,2,0:T(8,128)} %copy-done, f32[32,8,2,128]{3,1,2,0:T(8,128)S(1)} %collective-permute-done, f32[32,8,20,2]{3,1,2,0:T(8,128)} %copy.47, f32[32,8,2,128]{3,1,2,0:T(8,128)S(1)} %collective-permute-done.1, f32[32,8,20,2]{3,1,2,0:T(8,128)} %copy.45, ...), kind=kLoop, calls=%fused_computation.23 | loop fusion | flops 24117248 | bytes 9191424 | tf_op jit(solution)/shard_map/add | solution.py:61
  86.3 4.5 collective-permute-start.8
  90.8 1.9 collective-permute-start.9
  92.7 2.5 fusion.512
  95.2 3.3 collective-permute-done.9
  99.2 3.3 fusion.509
  102.5 2.9 copy.51
  105.4 3.6 collective-permute-start.10
  109.0 2.9 copy.52
  112.0 1.8 collective-permute-start.11
  115.0 3.4 copy.53
  118.4 3.4 copy.54
  121.8 9.1 %broadcast_multiply_fusion.2 = (f32[32,8,20,132]{3,1,2,0:T(8,128)}, f32[32,8,20,132]{3,1,2,0:T(8,128)}, f32[32,8,20,132]{3,1,2,0:T(8,128)}) fusion(f32[8,20,132]{2,0,1:T(8,128)} %copy.50, f32[32,8,20,2]{3,1,2,0:T(8,128)} %copy.54, f32[32,8,2,128]{3,1,2,0:T(8,128)} %copy-done.5, f32[32,8,16,128]{3,1,2,0:T(8,128)S(1)} %fusion.10, ...), kind=kLoop, calls=%fused_computation.8 | loop fusion | flops 4730880 | bytes 11066880 | tf_op jit(solution)/shard_map/mul | solution.py:73
  130.9 23.3 %convert_add_fusion = f32[32,8,16,128]{3,1,2,0:T(8,128)} fusion(f32[32,8,20,132]{3,1,2,0:T(8,128)} %get-tuple-element.2438, f32[32,8,20,132]{3,1,2,0:T(8,128)} %get-tuple-element.2437, f32[32,8,16,128]{3,1,2,0:T(8,128)S(1)} %fusion.10, f32[32,8,20,132]{3,1,2,0:T(8,128)} %get-tuple-element.2436, f32[32,1,16,128]{3,1,2,0:T(1,128)} %get-tuple-element.2444, ...), kind=kLoop, calls=%fused_computation.2 | loop fusion | flops 16777216 | bytes 36765696 | tf_op jit(solution)/shard_map/add | solution.py:132
  154.2 6.4 %fusion.40 = f32[32,32]{1,0:T(8,128)S(1)} fusion(f32[32,8,16,128]{3,1,2,0:T(8,128)} %convert_add_fusion), kind=kOutput, calls=%fused_computation.75 | convolution fusion | flops 201326592 | bytes 2101248 | tf_op jit(solution)/shard_map/dot_general | solution.py:135
  160.6 2.8 fusion.43
  163.4 86.3 %all-reduce.4 = (f32[32,32]{1,0:T(8,128)S(1)}, f32[32,32]{0,1:T(8,128)S(1)}) all-reduce(f32[32,32]{1,0:T(8,128)S(1)} %fusion.40, f32[32,32]{0,1:T(8,128)S(1)} %fusion.43), channel_id=1, replica_groups=mesh['row'=8,'col'=32] {'row','col'}, use_global_device_ids=true, to_apply=%region_1.0 | all-reduce | flops 2048 | bytes 16384 | tf_op jit(solution)/shard_map/psum | solution.py:137
  330.8 1.7 copy.60
  414.1 1.5 fusion.249
  417.1 1.4 fusion.253
  418.6 1.5 fusion.255
  420.1 1.5 fusion.257
  423.0 1.5 fusion.261
  424.6 1.4 fusion.263
  426.0 1.4 fusion.265
  427.5 1.4 fusion.267
  436.1 1.5 fusion.279
  437.6 1.5 fusion.281
  440.5 1.4 fusion.285
  442.0 1.4 fusion.287
  443.4 1.4 fusion.289
  444.9 1.4 fusion.291
  447.8 1.4 fusion.295
  452.3 1.4 fusion.173
  455.1 1.4 fusion.177
  458.0 1.4 fusion.181
  460.9 1.5 fusion.185
  465.2 1.5 fusion.191
  466.7 1.5 fusion.193
  468.2 1.4 fusion.195
  469.7 1.5 fusion.197
  472.6 1.5 fusion.201
  477.0 1.5 fusion.207
  478.5 1.5 fusion.209
  481.4 1.4 fusion.213
  484.3 1.4 fusion.217
  487.1 1.4 fusion.221
  490.1 1.4 fusion.225
  492.9 1.5 fusion.229
  498.3 3.0 fusion.37
  501.3 1.7 copy.67
  (645 shorter events, 191.6 us)
Async XLA Ops:
  1.5 8.8 %copy-start.7 = (f32[8,16,128]{2,1,0:T(8,128)S(1)}, f32[8,16,128]{2,1,0:T(8,128)}, u32[]{:S(2)}) copy-start(f32[8,16,128]{2,1,0:T(8,128)} %param.393) | copy-start | bytes 196612
  1.5 8.8 %copy-start.8 = (f32[8,16,128]{2,1,0:T(8,128)S(1)}, f32[8,16,128]{2,1,0:T(8,128)}, u32[]{:S(2)}) copy-start(f32[8,16,128]{2,1,0:T(8,128)} %param.392) | copy-start | bytes 196612
  1.5 8.8 %copy-start.9 = (f32[8,16,128]{2,1,0:T(8,128)S(1)}, f32[8,16,128]{2,1,0:T(8,128)}, u32[]{:S(2)}) copy-start(f32[8,16,128]{2,1,0:T(8,128)} %param.391) | copy-start | bytes 196612
  3.1 43.5 %copy-start = (f32[32,8,16,128]{3,1,2,0:T(8,128)}, f32[32,8,16,128]{3,1,2,0:T(8,128)S(1)}, u32[]{:S(2)}) copy-start(f32[32,8,16,128]{3,1,2,0:T(8,128)S(1)} %convert_multiply_fusion) | copy-start | bytes 6291460
  3.2 43.4 %collective-permute-start = (f32[32,8,2,128]{3,1,2,0:T(8,128)S(1)}, f32[32,8,2,128]{3,1,2,0:T(8,128)S(1)}, u32[]{:S(2)}, u32[]{:S(2)}) collective-permute-start(f32[32,8,2,128]{3,1,2,0:T(8,128)S(1)} %get-tuple-element.2454), channel_id=1, source_target_pairs={{32,0},{64,32},{96,64},{128,96},{160,128},{192,160},{224,192},{33,... | collective-permute-start | bytes 786440 | tf_op jit(solution)/shard_map/ppermute | solution.py:15
  8.4 38.3 %collective-permute-start.1 = (f32[32,8,2,128]{3,1,2,0:T(8,128)S(1)}, f32[32,8,2,128]{3,1,2,0:T(8,128)S(1)}, u32[]{:S(2)}, u32[]{:S(2)}) collective-permute-start(f32[32,8,2,128]{3,1,2,0:T(8,128)S(1)} %get-tuple-element.2453), channel_id=1, source_target_pairs={{0,32},{32,64},{64,96},{96,128},{128,160},{160,192},{192,224},{1,3... | collective-permute-start | bytes 786440 | tf_op jit(solution)/shard_map/ppermute | solution.py:12
  10.3 7.9 %collective-permute-start.4 = (f32[3,8,2,128]{3,2,1,0:T(2,128)S(1)}, f32[3,8,2,128]{3,2,1,0:T(2,128)S(1)}, u32[]{:S(2)}, u32[]{:S(2)}) collective-permute-start(f32[3,8,2,128]{3,2,1,0:T(2,128)S(1)} %get-tuple-element.2460), channel_id=1, source_target_pairs={{0,32},{32,64},{64,96},{96,128},{128,160},{160,192},{192,224},{1,3... | collective-permute-start | bytes 73736 | tf_op jit(solution)/shard_map/ppermute | solution.py:12
  12.3 6.0 %collective-permute-start.5 = (f32[3,8,2,128]{3,2,1,0:T(2,128)S(1)}, f32[3,8,2,128]{3,2,1,0:T(2,128)S(1)}, u32[]{:S(2)}, u32[]{:S(2)}) collective-permute-start(f32[3,8,2,128]{3,2,1,0:T(2,128)S(1)} %get-tuple-element.2461), channel_id=1, source_target_pairs={{32,0},{64,32},{96,64},{128,96},{160,128},{192,160},{224,192},{33,... | collective-permute-start | bytes 73736 | tf_op jit(solution)/shard_map/ppermute | solution.py:15
  18.5 26.9 %collective-permute-start.6 = (f32[3,8,20,2]{3,2,1,0:T(8,128)S(1)}, f32[3,8,20,2]{3,2,1,0:T(8,128)S(1)}, u32[]{:S(2)}, u32[]{:S(2)}) collective-permute-start(f32[3,8,20,2]{3,2,1,0:T(8,128)S(1)} %get-tuple-element.2458), channel_id=1, source_target_pairs={{0,1},{1,2},{2,3},{3,4},{4,5},{5,6},{6,7},{7,8},{8,9},{9,10},{10,1... | collective-permute-start | bytes 11528 | tf_op jit(solution)/shard_map/ppermute | solution.py:12
  21.1 24.3 %collective-permute-start.7 = (f32[3,8,20,2]{3,2,1,0:T(8,128)S(1)}, f32[3,8,20,2]{3,2,1,0:T(8,128)S(1)}, u32[]{:S(2)}, u32[]{:S(2)}) collective-permute-start(f32[3,8,20,2]{3,2,1,0:T(8,128)S(1)} %get-tuple-element.2459), channel_id=1, source_target_pairs={{1,0},{2,1},{3,2},{4,3},{5,4},{6,5},{7,6},{8,7},{9,8},{10,9},{11,1... | collective-permute-start | bytes 11528 | tf_op jit(solution)/shard_map/ppermute | solution.py:15
  22.4 391.0 %copy-start.4 = (f32[32,32]{1,0:T(8,128)}, f32[32,32]{1,0:T(8,128)S(1)}, u32[]{:S(2)}) copy-start(f32[32,32]{1,0:T(8,128)S(1)} %fusion.303) | copy-start | bytes 12292
  53.0 11.6 %collective-permute-start.2 = (f32[32,8,20,2]{0,1,3,2:T(8,128)}, f32[32,8,20,2]{0,1,3,2:T(8,128)}, u32[]{:S(2)}, u32[]{:S(2)}) collective-permute-start(f32[32,8,20,2]{0,1,3,2:T(8,128)} %copy.44), channel_id=1, source_target_pairs={{1,0},{2,1},{3,2},{4,3},{5,4},{6,5},{7,6},{8,7},{9,8},{10,9},{11,1... | collective-permute-start | bytes 122888 | tf_op jit(solution)/shard_map/ppermute | solution.py:15
  56.3 12.7 %collective-permute-start.3 = (f32[32,8,20,2]{0,1,3,2:T(8,128)}, f32[32,8,20,2]{0,1,3,2:T(8,128)S(1)}, u32[]{:S(2)}, u32[]{:S(2)}) collective-permute-start(f32[32,8,20,2]{0,1,3,2:T(8,128)} %copy.46), channel_id=1, source_target_pairs={{0,1},{1,2},{2,3},{3,4},{4,5},{5,6},{6,7},{7,8},{8,9},{9,10},{10,1... | collective-permute-start | bytes 122888 | tf_op jit(solution)/shard_map/ppermute | solution.py:12
  64.5 8.0 %copy-start.6 = (f32[32,1,16,128]{3,1,2,0:T(1,128)S(1)}, f32[32,1,16,128]{3,1,2,0:T(1,128)}, u32[]{:S(2)}) copy-start(f32[32,1,16,128]{3,1,2,0:T(1,128)} %get-tuple-element.2450) | copy-start | bytes 786436
  64.5 8.0 %copy-start.10 = (f32[8,16,128]{2,0,1:T(8,128)S(1)}, f32[8,16,128]{2,0,1:T(8,128)}, u32[]{:S(2)}) copy-start(f32[8,16,128]{2,0,1:T(8,128)} %copy.49) | copy-start | bytes 196612
  64.5 8.0 %copy-start.11 = (f32[8,16,128]{2,0,1:T(8,128)S(1)}, f32[8,16,128]{2,0,1:T(8,128)}, u32[]{:S(2)}) copy-start(f32[8,16,128]{2,0,1:T(8,128)} %copy.43) | copy-start | bytes 196612
  64.5 8.0 %copy-start.12 = (f32[8,16,128]{2,0,1:T(8,128)S(1)}, f32[8,16,128]{2,0,1:T(8,128)}, u32[]{:S(2)}) copy-start(f32[8,16,128]{2,0,1:T(8,128)} %copy.48) | copy-start | bytes 196612
  86.3 8.9 %collective-permute-start.8 = (f32[32,8,2,128]{3,1,2,0:T(8,128)S(1)}, f32[32,8,2,128]{3,1,2,0:T(8,128)S(1)}, u32[]{:S(2)}, u32[]{:S(2)}) collective-permute-start(f32[32,8,2,128]{3,1,2,0:T(8,128)S(1)} %get-tuple-element.2447), channel_id=1, source_target_pairs={{0,32},{32,64},{64,96},{96,128},{128,160},{160,192},{192,224},{1,3... | collective-permute-start | bytes 786440 | tf_op jit(solution)/shard_map/ppermute | solution.py:12
  90.8 7.7 %collective-permute-start.9 = (f32[32,8,2,128]{3,1,2,0:T(8,128)S(1)}, f32[32,8,2,128]{3,1,2,0:T(8,128)S(1)}, u32[]{:S(2)}, u32[]{:S(2)}) collective-permute-start(f32[32,8,2,128]{3,1,2,0:T(8,128)S(1)} %get-tuple-element.2448), channel_id=1, source_target_pairs={{32,0},{64,32},{96,64},{128,96},{160,128},{192,160},{224,192},{33,... | collective-permute-start | bytes 786440 | tf_op jit(solution)/shard_map/ppermute | solution.py:15
  98.5 0.7 copy-start.5
  105.4 9.6 %collective-permute-start.10 = (f32[32,8,20,2]{0,1,3,2:T(8,128)S(1)}, f32[32,8,20,2]{0,1,3,2:T(8,128)S(1)}, u32[]{:S(2)}, u32[]{:S(2)}) collective-permute-start(f32[32,8,20,2]{0,1,3,2:T(8,128)S(1)} %copy.51), channel_id=1, source_target_pairs={{0,1},{1,2},{2,3},{3,4},{4,5},{5,6},{6,7},{7,8},{8,9},{9,10},{10,1... | collective-permute-start | bytes 122888 | tf_op jit(solution)/shard_map/ppermute | solution.py:12
  112.0 6.4 %collective-permute-start.11 = (f32[32,8,20,2]{0,1,3,2:T(8,128)S(1)}, f32[32,8,20,2]{0,1,3,2:T(8,128)S(1)}, u32[]{:S(2)}, u32[]{:S(2)}) collective-permute-start(f32[32,8,20,2]{0,1,3,2:T(8,128)S(1)} %copy.52), channel_id=1, source_target_pairs={{1,0},{2,1},{3,2},{4,3},{5,4},{6,5},{7,6},{8,7},{9,8},{10,9},{11,1... | collective-permute-start | bytes 122888 | tf_op jit(solution)/shard_map/ppermute | solution.py:15
  121.8 9.1 %copy-start.2 = (bf16[32,8,16,128]{3,2,1,0:T(8,128)(2,1)S(1)}, bf16[32,8,16,128]{3,2,1,0:T(8,128)(2,1)}, u32[]{:S(2)}) copy-start(bf16[32,8,16,128]{3,2,1,0:T(8,128)(2,1)} %param.389) | copy-start | bytes 3145732
  154.2 6.4 %copy-start.1 = (f32[32,8,16,128]{3,1,2,0:T(8,128)S(1)}, f32[32,8,16,128]{3,1,2,0:T(8,128)}, u32[]{:S(2)}) copy-start(f32[32,8,16,128]{3,1,2,0:T(8,128)} %convert_add_fusion) | copy-start | bytes 6291460
  332.5 165.8 %copy-start.3 = (f32[32,8,16,128]{3,2,1,0:T(8,128)S(1)}, f32[32,8,16,128]{3,2,1,0:T(8,128)}, u32[]{:S(2)}) copy-start(f32[32,8,16,128]{3,2,1,0:T(8,128)} %copy.60) | copy-start | bytes 6291460
where the time goes:
time: 513 us; the launch traced here: 503 us
  local copies, waits for them, and re-layouts  116 us (23%)
  other arithmetic  111 us (22%)
  matrix products  108 us (21%)
  blocking collectives  86.3 us (17%)
  between operations  45.7 us (9%)
  starting transfers between devices  33.3 us (6%)
    psum x1, blocking collectives, shards(): gram, core = lax.psum((gram_part, core_part), ('row', 'col'))  86.3 us
    dot_general x64, matrix products, lower_inverse(): jnp.dot(lower[row_id], result, precision=lax.Precision.HIGHEST)  86.2 us
    another operation x157, other arithmetic  61.4 us
    slice x62, local copies, waits for them, and re-layouts, lower_chol(): pivot = jnp.sqrt(resid[col_id])  36.9 us
    add x1, other arithmetic, shards(): sketch = omega + spread * back  23.3 us
    ppermute x6, starting transfers between devices, padded_2(): lax.ppermute(lax.slice_in_dim(block, block.shape[dim] - width, None, axis...  19.4 us
    ppermute x6, starting transfers between devices, padded_2(): lax.ppermute(lax.slice_in_dim(block, 0, width, axis=dim), axis, backward)  13.9 us
    add x1, other arithmetic, tangent(): center + coef_x * first_diff(padded, 0) + coef_y * first_diff(padded, 1)  13.8 us
  transfers between devices with their start and end apart: 12, of which 1 were waited for; matrix products, arithmetic and copies ran while one was open for 9% of the time, Pallas kernels for 0%

commit v1 on v0

v1 whole, which is shorter than its diff:
```python
import functools

import jax
import jax.numpy as jnp
from jax import lax
from jax.experimental import pallas as pl
from jax.experimental.pallas import tpu as pltpu
from jax.sharding import PartitionSpec as P

MESH = pl.DeviceIdType.MESH
F32 = jnp.float32
BF16 = jnp.bfloat16
INNER = 4
NF = 8
SPR, CEN, XP, XM, XA, YP, YM, YA = range(NF)
LOW, HIGH, LEFT, RIGHT = range(4)


def lanes(shape):
    return lax.broadcasted_iota(jnp.int32, shape, 1)


def roll(x, shift):
    return pltpu.roll(x, shift % 128, 1)


def put_row(ref, r, value):
    n, rows, width = ref.shape
    ref.reshape(n * rows, width)[pl.ds(r, n, stride=rows), :] = value


def wide(coef, nprobe):
    return jnp.broadcast_to(coef[None], (nprobe // 8, 8, 128)).reshape(nprobe, 128)


def halo_kernel(
    dims,
    probes_hbm, spread_hbm, advx_hbm, advy_hbm, diff_hbm,
    z_hbm, g_ref,
    probes, coefs, turn, omega, scaled, tang, co, edge,
    pack, pack_l, pack_r, wrap, wrap_l, wrap_r,
    to_low, to_high, from_low, from_high,
    zbuf, gbuf, red0, red1, red2,
    in_sem, out_sem, send_sem, recv_sem, red_send, red_recv,
):
    nprobe, nlev, nrow, nrd, ncd = dims
    outer = ncd // INNER
    row = lax.axis_index("row")
    col = lax.axis_index("col")
    zi = col // INNER
    xi = lax.rem(col, INNER)
    half = nprobe // 2

    loads = []
    for i, src in enumerate((spread_hbm, advx_hbm, advy_hbm, diff_hbm)):
        loads.append(pltpu.make_async_copy(src, coefs.at[i], in_sem.at[i]))
    loads.append(pltpu.make_async_copy(probes_hbm, probes, in_sem.at[4]))
    for load in loads:
        load.start()

    barrier = pltpu.get_barrier_semaphore()
    for o in range(1, nrd):
        pl.semaphore_signal(barrier, inc=1, device_id=(lax.rem(row + o, nrd), col), device_id_type=MESH)
    for o in range(1, INNER):
        pl.semaphore_signal(
            barrier, inc=1, device_id=(row, zi * INNER + lax.rem(xi + o, INNER)), device_id_type=MESH
        )
    for o in range(1, outer):
        pl.semaphore_signal(
            barrier, inc=1, device_id=(row, lax.rem(zi + o, outer) * INNER + xi), device_id_type=MESH
        )
    for o in (1, ncd - 1):
        pl.semaphore_signal(barrier, inc=1, device_id=(row, lax.rem(col + o, ncd)), device_id_type=MESH)

    for load in loads[:4]:
        load.wait()

    def spread_coefs(l, carry):
        ax = coefs[1, l] * (1.0 / 12.0)
        ay = coefs[2, l] * (1.0 / 12.0)
        d = coefs[3, l]
        fields = (coefs[0, l], 0.6 - 4.0 * d, d + 8.0 * ax, d - 8.0 * ax, ax, d + 8.0 * ay, d - 8.0 * ay, ay)
        for f in range(NF):
            for r in range(nrow):
                co[f, l, r] = jnp.broadcast_to(fields[f][r : r + 1], (8, 128))
        return carry

    lax.fori_loop(0, nlev, spread_coefs, 0)

    lane16 = lanes((half, 128))
    quad = lax.rem(lane16, 4)
    lane_l = lanes((nlev, 128))
    quad_l = lax.rem(lane_l, 4)

    def packed(field):
        acc = jnp.zeros((nlev, 128), F32)
        for r in range(nrow):
            acc = jnp.where(lax.div(lane_l, 4) == r, roll(coefs[field, :, r, :], 4 * r + 2), acc)
        return jnp.where(lane_l < 64, acc, roll(acc, 64))

    pa = packed(2) * (1.0 / 12.0)
    pd = packed(3)
    edge[0] = jnp.where(quad_l == 1, pd + 8.0 * pa, jnp.where(quad_l == 2, pd - 8.0 * pa, 0.0))
    edge[1] = pa

    has = {LOW: row > 0, HIGH: row < nrd - 1, LEFT: col > 0, RIGHT: col < ncd - 1}
    target = {LOW: (row - 1, col), HIGH: (row + 1, col), LEFT: (row, col - 1), RIGHT: (row, col + 1)}
    rims = (
        {
            LOW: (lambda l: scaled.at[l, 2:4], lambda l: scaled.at[l, nrow + 2 : nrow + 4]),
            HIGH: (lambda l: scaled.at[l, nrow : nrow + 2], lambda l: scaled.at[l, 0:2]),
            LEFT: (lambda l: pack.at[l], lambda l: pack_r.at[l]),
            RIGHT: (lambda l: pack.at[l], lambda l: pack_l.at[l]),
        },
        {
            LOW: (lambda l: to_low.at[l], lambda l: from_high.at[l]),
            HIGH: (lambda l: to_high.at[l], lambda l: from_low.at[l]),
            LEFT: (lambda l: wrap.at[l], lambda l: wrap_r.at[l]),
            RIGHT: (lambda l: wrap.at[l], lambda l: wrap_l.at[l]),
        },
    )
    opposite = {LOW: HIGH, HIGH: LOW, LEFT: RIGHT, RIGHT: LEFT}

    def rim(phase, side, l):
        src, dst = rims[phase][side]
        return pltpu.make_async_remote_copy(
            src_ref=src(l),
            dst_ref=dst(l),
            send_sem=send_sem.at[phase, side, l],
            recv_sem=recv_sem.at[phase, side, l],
            device_id=target[side],
            device_id_type=MESH,
        )

    def send(phase, l):
        for side in (LOW, HIGH, LEFT, RIGHT):
            @pl.when(has[side])
            def _():
                rim(phase, side, l).start()

    def receive(phase, l):
        for side in (LEFT, RIGHT, LOW, HIGH):
            @pl.when(has[side])
            def _():
                rim(phase, opposite[side], l).wait_recv()

    def sent(phase, l):
        for side in (LOW, HIGH, LEFT, RIGHT):
            @pl.when(has[side])
            def _():
                rim(phase, side, l).wait_send()

    zero_rows = jnp.zeros((nlev, 2, nprobe, 128), F32)
    zero_pack = jnp.zeros((nlev, half, 128), F32)

    @pl.when(row == 0)
    def _():
        scaled[:, 0:2] = zero_rows
        from_low[...] = zero_rows

    @pl.when(row == nrd - 1)
    def _():
        scaled[:, nrow + 2 : nrow + 4] = zero_rows
        from_high[...] = zero_rows

    @pl.when(col == 0)
    def _():
        pack_l[...] = zero_pack
        wrap_l[...] = zero_pack

    @pl.when(col == ncd - 1)
    def _():
        pack_r[...] = zero_pack
        wrap_r[...] = zero_pack

    loads[4].wait()
    pl.semaphore_wait(barrier, (nrd - 1) + (INNER - 1) + (outer - 1) + 2)

    def put(acc, r, value):
        slot = lax.div(lane16, 4)
        acc = jnp.where(slot == r, roll(value[:half], 4 * r + 2), acc)
        return jnp.where(slot == r + 16, roll(value[half:], 4 * r + 66), acc)

    wide_lane = lanes((nprobe, 128))
    at_edge = jnp.logical_or(wide_lane < 2, wide_lane >= 126)

    def take(corr, r):
        both = jnp.concatenate([roll(corr, -(4 * r + 2)), roll(corr, -(4 * r + 66))], axis=0)
        return jnp.where(at_edge, both, 0.0)

    def scale_level(l, carry):
        for p in range(nprobe):
            turn[p * nrow : (p + 1) * nrow, :] = probes[p, l].astype(F32)
        acc = jnp.zeros((half, 128), F32)
        for r in range(nrow):
            om = turn[pl.ds(r, nprobe, stride=nrow), :]
            omega[l, r] = om.astype(BF16)
            v = om * wide(co[SPR, l, r], nprobe)
            scaled[l, r + 2] = v
            acc = put(acc, r, v)
        pack[l] = acc
        send(0, l)
        return carry

    lax.fori_loop(0, nlev, scale_level, 0)

    def tangent_level(l, carry):
        receive(0, l)
        above = jnp.minimum(l + 1, nlev - 1)
        below = jnp.maximum(l - 1, 0)
        e1 = edge[0, pl.ds(l, 1), :]
        ea = edge[1, pl.ds(l, 1), :]
        diff = jnp.where(quad < 2, pack_l[l], pack_r[l]) - pack[l]
        near = jnp.where(quad == 1, roll(diff, -1), roll(diff, 1))
        far = jnp.where(quad < 2, -roll(diff, -2), roll(diff, 2))
        corr = e1 * near + ea * far
        acc = jnp.zeros((half, 128), F32)
        rims_of = {}
        for r in range(nrow):
            c = [wide(co[f, l, r], nprobe) for f in range(NF)]
            v = scaled[l, r + 2]
            t = c[CEN] * v + 0.2 * (scaled[above, r + 2] + scaled[below, r + 2])
            t = t + c[XP] * scaled[l, r + 3] + c[XM] * scaled[l, r + 1]
            t = t + c[XA] * (scaled[l, r] - scaled[l, r + 4])
            t = t + c[YP] * roll(v, -1) + c[YM] * roll(v, 1) + c[YA] * (roll(v, 2) - roll(v, -2))
            t = t + take(corr, r)
            tang[l, r] = t
            acc = put(acc, r, t)
            if r == 0:
                to_low[l, 0] = c[XA] * t
                rims_of[r] = c[XM] * t
            if r == 1:
                to_low[l, 1] = rims_of[0] + c[XA] * t
            if r == nrow - 2:
                rims_of[r] = c[XA] * t
            if r == nrow - 1:
                to_high[l, 0] = c[XP] * t - rims_of[nrow - 2]
                to_high[l, 1] = -(c[XA] * t)
        u = ea * acc
        w = e1 * acc
        wrap[l] = jnp.where(quad < 2, roll(u, -2), -roll(u, 2)) + jnp.where(
            quad == 1, roll(w, -1), jnp.where(quad == 2, roll(w, 1), 0.0)
        )
        send(1, l)
        return carry

    lax.fori_loop(0, nlev, tangent_level, 0)

    def adjoint_level(l, gram):
        receive(1, l)
        above = jnp.minimum(l + 1, nlev - 1)
        below = jnp.maximum(l - 1, 0)
        corr = jnp.where(quad < 2, wrap_r[l], wrap_l[l]) - wrap[l]
        for r0 in range(0, nrow, 2):
            left, right = [], []
            for r in (r0, r0 + 1):
                c = [wide(co[f, l, r], nprobe) for f in (CEN, YP, YM, YA, SPR)]
                w = tang[l, r]
                b = c[0] * w + 0.2 * (tang[above, r] + tang[below, r])
                if r + 1 < nrow:
                    b = b + wide(co[XM, l, r + 1], nprobe) * tang[l, r + 1]
                if r >= 1:
                    b = b + wide(co[XP, l, r - 1], nprobe) * tang[l, r - 1]
                if r + 2 < nrow:
                    b = b + wide(co[XA, l, r + 2], nprobe) * tang[l, r + 2]
                if r >= 2:
                    b = b - wide(co[XA, l, r - 2], nprobe) * tang[l, r - 2]
                ya = c[3] * w
                b = b + roll(c[2] * w, -1) + roll(c[1] * w, 1) + (roll(ya, -2) - roll(ya, 2))
                if r < 2:
                    b = b + from_low[l, r]
                if r >= nrow - 2:
                    b = b + from_high[l, r - (nrow - 2)]
                b = b + take(corr, r)
                om = omega[l, r]
                sk = om.astype(F32) + c[4] * b
                hi = sk.astype(BF16)
                lo = (sk - hi.astype(F32)).astype(BF16)
                z = jnp.concatenate([hi, lo], axis=0)
                zbuf[l, r] = z
                right.append(z)
                left.append(jnp.concatenate([z, om], axis=0))
            gram = gram + lax.dot_general(
                jnp.concatenate(left, axis=1),
                jnp.concatenate(right, axis=1),
                (((1,), (1,)), ((), ())),
                preferred_element_type=F32,
            )
        pltpu.make_async_copy(zbuf.at[l], z_hbm.at[l], out_sem.at[l]).start()
        return gram

    gram = lax.fori_loop(0, nlev, adjoint_level, jnp.zeros((3 * nprobe, 2 * nprobe), F32))

    gbuf[...] = jnp.zeros(gbuf.shape, F32)
    gbuf[:, 0 : 2 * nprobe] = gram
    full = gbuf[...]
    full = full + roll(full, -nprobe)
    own = full[:nprobe] + full[nprobe : 2 * nprobe]
    both = jnp.where(wide_lane < nprobe, own, roll(full[2 * nprobe :], nprobe))
    part = jnp.where(lane16 < 64, both[:half], roll(both[half:], 64))

    stages = (
        (red0, nrd, row, lambda t: (t, col)),
        (red1, INNER, xi, lambda t: (row, zi * INNER + t)),
        (red2, outer, zi, lambda t: (row, t * INNER + xi)),
    )
    copies = []
    for s, (buf, count, me, at) in enumerate(stages):
        buf[me] = part
        stage = []
        for o in range(1, count):
            stage.append(
                pltpu.make_async_remote_copy(
                    src_ref=buf.at[me],
                    dst_ref=buf.at[me],
                    send_sem=red_send.at[s, o],
                    recv_sem=red_recv.at[s, o],
                    device_id=at(lax.rem(me + o, count)),
                    device_id_type=MESH,
                )
            )
            stage[-1].start()
        for copy in stage:
            copy.wait_recv()
        part = buf[0]
        for o in range(1, count):
            part = part + buf[o]
        copies += stage
    g_ref[...] = part

    for copy in copies:
        copy.wait_send()

    def finish(l, carry):
        sent(0, l)
        sent(1, l)
        pltpu.make_async_copy(zbuf.at[l], z_hbm.at[l], out_sem.at[l]).wait()
        return carry

    lax.fori_loop(0, nlev, finish, 0)


def basis_kernel(nprobe, nlev, nrow, scale, g_ref, z_hbm, basis_hbm, factor_ref, zbuf, obuf, in_sem, out_sem):
    def load(l):
        return pltpu.make_async_copy(z_hbm.at[l], zbuf.at[l], in_sem.at[l])

    def store(l):
        return pltpu.make_async_copy(obuf.at[l], basis_hbm.at[:, l], out_sem.at[l])

    for l in range(nlev):
        load(l).start()
    half = nprobe // 2
    g = g_ref[...]
    both = jnp.concatenate([g, roll(g, 64)], axis=0)
    flip = both.T
    lane = lanes((nprobe, 128))
    sub = lax.broadcasted_iota(jnp.int32, (nprobe, 128), 0)
    pad = jnp.zeros((nprobe, 128 - nprobe), F32)
    flip_g = jnp.concatenate([flip[:nprobe], pad], axis=1)
    flip_c = jnp.concatenate([flip[nprobe : 2 * nprobe], pad], axis=1)
    sym_g = 0.5 * (both + flip_g)
    sym_c = 0.5 * (roll(both, -nprobe) + flip_c)
    m = jnp.where(lane < nprobe, sym_g, jnp.where(jnp.logical_and(lane >= 64, lane < 64 + nprobe), roll(sym_c, 64), 0.0))
    m = jnp.where(jnp.logical_or(lane == sub + nprobe, lane == sub + 64 + nprobe), 1.0, m)
    first = lane < 64
    piv = jnp.ones((nprobe, 128), F32)
    for k in range(nprobe):
        col = jnp.where(first, m[:, k : k + 1], m[:, 64 + k : 65 + k])
        p = col[k : k + 1]
        line = m[k : k + 1] / p
        piv = jnp.where(sub == k, p, piv)
        m = jnp.where(sub > k, m - col * line, m)
    m = m * (1.0 / jnp.sqrt(piv))
    upper = jnp.where(jnp.logical_and(lane >= sub, lane < nprobe), m, 0.0)
    inv_g = jnp.where(lane <= sub, roll(m, -nprobe), 0.0)
    inv_c = jnp.where(lane <= sub, roll(m, -(64 + nprobe)), 0.0)
    factor = lax.dot_general(
        upper, inv_c, (((1,), (1,)), ((), ())), precision=lax.Precision.HIGHEST, preferred_element_type=F32
    )
    factor_ref[...] = factor
    a = inv_g * scale
    a_hi = a.astype(BF16)
    a_lo = (a - a_hi.astype(F32)).astype(BF16)
    twice = jnp.where(lane < nprobe, a_hi.astype(F32), roll(a_hi.astype(F32), nprobe))
    twice_lo = jnp.where(lane < nprobe, a_lo.astype(F32), roll(a_lo.astype(F32), nprobe))
    lhs = jnp.concatenate([twice, twice_lo], axis=0).astype(BF16)[:, : 2 * nprobe]

    def level(l, carry):
        load(l).wait()
        for r in range(nrow):
            out = lax.dot_general(
                lhs, zbuf[l, r], (((1,), (0,)), ((), ())), preferred_element_type=F32
            )
            put_row(obuf.at[l], r, out[:nprobe] + out[nprobe:])
        store(l).start()
        return carry

    lax.fori_loop(0, nlev, level, 0)

    def finish(l, carry):
        store(l).wait()
        return carry

    lax.fori_loop(0, nlev, finish, 0)


def shards(probes, spread, adv_x, adv_y, diffusivity):
    nprobe, nlev, nrow, ncol = probes.shape
    nrd = lax.axis_size("row")
    ncd = lax.axis_size("col")
    half = nprobe // 2
    any_spec = pl.BlockSpec(memory_space=pl.ANY)
    vmem_spec = pl.BlockSpec(memory_space=pltpu.VMEM)
    rows2 = pltpu.VMEM((nlev, 2, nprobe, ncol), F32)
    strip = pltpu.VMEM((nlev, half, ncol), F32)
    most = max(nrd, INNER, ncd // INNER)
    z, g = pl.pallas_call(
        functools.partial(halo_kernel, (nprobe, nlev, nrow, nrd, ncd)),
        out_shape=(
            jax.ShapeDtypeStruct((nlev, nrow, 2 * nprobe, ncol), BF16),
            jax.ShapeDtypeStruct((half, ncol), F32),
        ),
        in_specs=[any_spec] * 5,
        out_specs=(any_spec, vmem_spec),
        scratch_shapes=[
            pltpu.VMEM((nprobe, nlev, nrow, ncol), BF16),
            pltpu.VMEM((4, nlev, nrow, ncol), F32),
            pltpu.VMEM((nprobe * nrow, ncol), F32),
            pltpu.VMEM((nlev, nrow, nprobe, ncol), BF16),
            pltpu.VMEM((nlev, nrow + 4, nprobe, ncol), F32),
            pltpu.VMEM((nlev, nrow, nprobe, ncol), F32),
            pltpu.VMEM((NF, nlev, nrow, 8, ncol), F32),
            pltpu.VMEM((2, nlev, ncol), F32),
            strip, strip, strip, strip, strip, strip,
            rows2, rows2, rows2, rows2,
            pltpu.VMEM((nlev, nrow, 2 * nprobe, ncol), BF16),
            pltpu.VMEM((3 * nprobe, ncol), F32),
            pltpu.VMEM((nrd, half, ncol), F32),
            pltpu.VMEM((INNER, half, ncol), F32),
            pltpu.VMEM((ncd // INNER, half, ncol), F32),
            pltpu.SemaphoreType.DMA((5,)),
            pltpu.SemaphoreType.DMA((nlev,)),
            pltpu.SemaphoreType.DMA((2, 4, nlev)),
            pltpu.SemaphoreType.DMA((2, 4, nlev)),
            pltpu.SemaphoreType.DMA((3, most)),
            pltpu.SemaphoreType.DMA((3, most)),
        ],
        compiler_params=pltpu.CompilerParams(
            collective_id=0, has_side_effects=True, vmem_limit_bytes=40 * 1024 * 1024
        ),
        name="sketch_and_sums",
    )(probes, spread, adv_x, adv_y, diffusivity)
    scale = float(nlev * nrow * ncol * nrd * ncd) ** 0.5
    basis, factor = pl.pallas_call(
        functools.partial(basis_kernel, nprobe, nlev, nrow, scale),
        out_shape=(
            jax.ShapeDtypeStruct((nprobe, nlev, nrow, ncol), F32),
            jax.ShapeDtypeStruct((nprobe, nprobe), F32),
        ),
        in_specs=[vmem_spec, any_spec],
        out_specs=(any_spec, vmem_spec),
        scratch_shapes=[
            pltpu.VMEM((nlev, nrow, 2 * nprobe, ncol), BF16),
            pltpu.VMEM((nlev, nprobe, nrow, ncol), F32),
            pltpu.SemaphoreType.DMA((nlev,)),
            pltpu.SemaphoreType.DMA((nlev,)),
        ],
        compiler_params=pltpu.CompilerParams(vmem_limit_bytes=24 * 1024 * 1024),
        name="factors_and_basis",
    )(g, z)
    return basis, factor


def solution(mesh):
    return jax.shard_map(
        shards,
        mesh=mesh,
        in_specs=(
            P(None, None, "row", "col"),
            P(None, "row", "col"),
            P(None, "row", "col"),
            P(None, "row", "col"),
            P(None, "row", "col"),
        ),
        out_specs=(P(None, None, "row", "col"), P()),
        check_vma=False,
    )
```

time: 513 us -> 53.4 us (0.10); the launches traced: 503 us -> 52.5 us
  local copies, waits for them, and re-layouts: 116 us -> 4.57 us
  other arithmetic: 111 us -> 0 us
  matrix products: 108 us -> 0 us
  blocking collectives: 86.3 us -> 0 us
  Pallas kernels: 0 us -> 47.3 us
  between operations: 45.7 us -> 0.65 us
  starting transfers between devices: 33.3 us -> 0 us
    dot_general x131 -> x0, matrix products: 108 us -> none  [the longest x64 86.2 us: lower_inverse(): jnp.dot(lower[row_id], result, precision=lax.Precision.HIGHEST)]
    psum x1 -> x0, blocking collectives: 86.3 us -> none  [shards(): gram, core = lax.psum((gram_part, core_part), ('row', 'col'))]
    slice x149 -> x0, local copies, waits for them, and re-layouts: 79.6 us -> none  [the longest x62 36.9 us: lower_chol(): pivot = jnp.sqrt(resid[col_id])]
    another operation x157 -> x0, other arithmetic: 61.4 us -> none
    pallas_call x0 -> x2, Pallas kernels: none -> 47.3 us  [the longest x1 40.6 us: shards(): pl.pallas_call(functools.partial(halo_kernel, (nprobe, nlev, nrow, nrd, n...]
    add x2 -> x0, other arithmetic: 37 us -> none  [the longest x1 23.3 us: shards(): sketch = omega + spread * back]
    ppermute x12 -> x0, starting transfers between devices: 33.3 us -> none  [the longest x6 19.4 us: padded_2(): lax.ppermute(lax.slice_in_dim(block, block.shape[dim] - width, None, axis...]
    ppermute x4 -> x0, local copies, waits for them, and re-layouts: 14.8 us -> none  [the longest x2 7.88 us: padded_2(): lax.ppermute(lax.slice_in_dim(block, 0, width, axis=dim), axis, backward)]
  transfers between devices with their start and end apart: 12 -> 0, of which waited for: 1 -> 0; matrix products, arithmetic and copies ran while one was open for 9% -> 0% of each run, Pallas kernels for 0% -> 0%
where the time goes in v1:
time: 53.4 us; the launch traced here: 52.5 us
  Pallas kernels  47.3 us (89%)
  local copies, waits for them, and re-layouts  4.57 us (9%)
  between operations  0.65 us (1%)
    pallas_call x1, Pallas kernels, shards(): pl.pallas_call(functools.partial(halo_kernel, (nprobe, nlev, nrow, nrd, n...  40.6 us
    pallas_call x1, Pallas kernels, shards(): pl.pallas_call(functools.partial(basis_kernel, nprobe, nlev, nrow, scale)...  6.64 us
    unnamed x10, local copies, waits for them, and re-layouts  4.57 us

profile of v1, /device:TPU:1, one launch (start us, length us, event | category | flops | bytes accessed | tf_op | source)
XLA Modules:
  0.0 52.5 jit_solution(9900624132048256477)
XLA Ops:
  0.6 0.0 copy-start
  0.6 1.2 %copy-done = bf16[32,8,16,128]{3,2,1,0:T(8,128)(2,1)S(1)} copy-done((bf16[32,8,16,128]{3,2,1,0:T(8,128)(2,1)S(1)}, bf16[32,8,16,128]{3,2,1,0:T(8,128)(2,1)}, u32[]{:S(2)}) %copy-start) | copy-done | bytes 1048600
  1.9 0.0 copy-start.1
  1.9 0.8 %copy-done.1 = f32[8,16,128]{2,1,0:T(8,128)S(1)} copy-done((f32[8,16,128]{2,1,0:T(8,128)S(1)}, f32[8,16,128]{2,1,0:T(8,128)}, u32[]{:S(2)}) %copy-start.1) | copy-done | bytes 65560
  2.7 0.0 copy-start.2
  2.7 0.8 %copy-done.2 = f32[8,16,128]{2,1,0:T(8,128)S(1)} copy-done((f32[8,16,128]{2,1,0:T(8,128)S(1)}, f32[8,16,128]{2,1,0:T(8,128)}, u32[]{:S(2)}) %copy-start.2) | copy-done | bytes 65560
  3.5 0.0 copy-start.3
  3.5 0.8 %copy-done.3 = f32[8,16,128]{2,1,0:T(8,128)S(1)} copy-done((f32[8,16,128]{2,1,0:T(8,128)S(1)}, f32[8,16,128]{2,1,0:T(8,128)}, u32[]{:S(2)}) %copy-start.3) | copy-done | bytes 65560
  4.4 0.0 copy-start.4
  4.4 0.8 %copy-done.4 = f32[8,16,128]{2,1,0:T(8,128)S(1)} copy-done((f32[8,16,128]{2,1,0:T(8,128)S(1)}, f32[8,16,128]{2,1,0:T(8,128)}, u32[]{:S(2)}) %copy-start.4) | copy-done | bytes 65560
  5.2 40.6 %sketch_and_sums.1 = (bf16[8,16,64,128]{3,2,1,0:T(8,128)(2,1)S(1)}, f32[16,128]{1,0:T(8,128)S(1)}) custom-call(bf16[32,8,16,128]{3,2,1,0:T(8,128)(2,1)S(1)} %copy-done, f32[8,16,128]{2,1,0:T(8,128)S(1)} %copy-done.1, f32[8,16,128]{2,1,0:T(8,128)S(1)} %copy-done.2, f32[8,16,128]{2,1,0:T(8,128)S(1)} %copy-done.3, f32[8,16,128]{2,1,0:T(8,128)S(1)} %copy-done.4), custom_call_target="tpu_custom_call" | custom-call | tf_op jit(solution)/shard_map/sketch_and_sums/pallas_call | solution.py:417
  45.8 6.6 %factors_and_basis.1 = (f32[32,8,16,128]{3,2,1,0:T(8,128)}, f32[32,32]{1,0:T(8,128)}) custom-call(f32[16,128]{1,0:T(8,128)S(1)} %get-tuple-element.4.g_ref, bf16[8,16,64,128]{3,2,1,0:T(8,128)(2,1)S(1)} %get-tuple-element.5.z_hbm), custom_call_target="tpu_custom_call" | custom-call | tf_op jit(solution)/shard_map/factors_and_basis/pallas_call | solution.py:454
Async XLA Ops:
  0.6 1.2 %copy-start = (bf16[32,8,16,128]{3,2,1,0:T(8,128)(2,1)S(1)}, bf16[32,8,16,128]{3,2,1,0:T(8,128)(2,1)}, u32[]{:S(2)}) copy-start(bf16[32,8,16,128]{3,2,1,0:T(8,128)(2,1)} %probes_hbm.1) | copy-start | bytes 3145732
  1.9 0.8 %copy-start.1 = (f32[8,16,128]{2,1,0:T(8,128)S(1)}, f32[8,16,128]{2,1,0:T(8,128)}, u32[]{:S(2)}) copy-start(f32[8,16,128]{2,1,0:T(8,128)} %spread_hbm.1) | copy-start | bytes 196612
  2.7 0.8 %copy-start.2 = (f32[8,16,128]{2,1,0:T(8,128)S(1)}, f32[8,16,128]{2,1,0:T(8,128)}, u32[]{:S(2)}) copy-start(f32[8,16,128]{2,1,0:T(8,128)} %advx_hbm.1) | copy-start | bytes 196612
  3.5 0.8 %copy-start.3 = (f32[8,16,128]{2,1,0:T(8,128)S(1)}, f32[8,16,128]{2,1,0:T(8,128)}, u32[]{:S(2)}) copy-start(f32[8,16,128]{2,1,0:T(8,128)} %advy_hbm.1) | copy-start | bytes 196612
  4.4 0.8 %copy-start.4 = (f32[8,16,128]{2,1,0:T(8,128)S(1)}, f32[8,16,128]{2,1,0:T(8,128)}, u32[]{:S(2)}) copy-start(f32[8,16,128]{2,1,0:T(8,128)} %diff_hbm.1) | copy-start | bytes 196612
